TPU v7x, 512 devices: a whole 4x4x16 slice. The times are simulated.
512 devices in a mesh: wide: 64 (over y, z_lo, x), narrow: 8 (over z_hi, core).
Axes of the slice: x: 4, y: 4, z: 16 (z_hi: 4, z_lo: 4; z = z_hi * 4 + z_lo), core: 2. Of those that a mesh axis runs over, the one named last changes fastest.
Arguments:
- inputs: bfloat16 [512, 6144], P('wide', 'narrow'), may hold values from -6 to 6
- upstream_output_gradient: bfloat16 [512, 6144], P('wide', 'narrow'), may hold values from -6 to 6
- input_weight_frozen: bfloat16 [6144, 24576], P('narrow', 'wide'), may hold values from -0.078125 to 0.078125
- output_weight_frozen: bfloat16 [24576, 6144], P('wide', 'narrow'), may hold values from -0.0390625 to 0.0390625
- input_down_factor: bfloat16 [64, 6144], P(None, 'narrow'), may hold values from -0.078125 to 0.078125
- input_up_factor: bfloat16 [64, 24576], P(None, 'wide'), may hold values from -0.0390625 to 0.0390625
- output_down_factor: bfloat16 [64, 24576], P(None, 'wide'), may hold values from -0.0390625 to 0.0390625
- up_out: bfloat16 [64, 6144], P(None, 'narrow'), may hold values from -0.078125 to 0.078125
Outputs:
- gradient_input_rows: bfloat16 [512, 6144], P('wide', 'narrow')
- input_down_gradient: float32 [64, 6144], P(None, 'narrow')
- input_up_gradient: float32 [64, 24576], P(None, 'wide')
- output_down_gradient: float32 [64, 24576], P(None, 'wide')
- output_up_gradient: float32 [64, 6144], P(None, 'narrow')
All inputs are finite; a program needn't handle non-finite values.
Results may differ from a plain program's by a relative error of at most 0.0051.
Values may be sent and summed in bfloat16 or wider, within the bound.
A program may use at most 64 MiB of HBM per device.

v0:
```python
import math

import jax
import jax.numpy as jnp
from jax import lax
from jax.sharding import PartitionSpec as P

adapter_scaling = 2.0
gelu_coef = math.sqrt(2.0 / math.pi)


def gelu_value(value):
    inner = jnp.tanh(gelu_coef * (value + 0.044715 * value * value * value))
    return 0.5 * value * (1.0 + inner)


def gelu_slope(value):
    inner = jnp.tanh(gelu_coef * (value + 0.044715 * value * value * value))
    return 0.5 * (1.0 + inner) + 0.5 * value * (1.0 - inner * inner) * gelu_coef * (
        1.0 + 3.0 * 0.044715 * value * value
    )


def times_t(left, right):
    return lax.dot_general(
        left, right, (((1,), (1,)), ((), ())), preferred_element_type=jnp.float32
    )


def transposed_product(left, right):
    return lax.dot_general(
        left, right, (((0,), (0,)), ((), ())), preferred_element_type=jnp.float32
    )


def activate(
    hidden_total,
    input_rank_product,
    gradient_total,
    gradient_rank_product,
    input_up_factor,
    output_down_factor,
):
    hidden_preactivation = hidden_total + adapter_scaling * jnp.dot(
        input_rank_product, input_up_factor, preferred_element_type=jnp.float32
    )
    activated_hidden = gelu_value(hidden_preactivation).astype(jnp.bfloat16)
    activated_gradient = gradient_total + adapter_scaling * jnp.dot(
        gradient_rank_product, output_down_factor, preferred_element_type=jnp.float32
    )
    preactivation_gradient = (activated_gradient * gelu_slope(hidden_preactivation)).astype(
        jnp.bfloat16
    )
    return (activated_hidden, preactivation_gradient)


def shards(
    inputs,
    upstream_output_gradient,
    input_weight_frozen,
    output_weight_frozen,
    input_down_factor,
    input_up_factor,
    output_down_factor,
    up_out,
):
    tok_rows = inputs.shape[0]
    strip_input, strip_gradient = (
        lax.all_gather(inputs, "wide", axis=0, tiled=True),
        lax.all_gather(upstream_output_gradient, "wide", axis=0, tiled=True),
    )
    h_part = jnp.dot(strip_input, input_weight_frozen, preferred_element_type=jnp.float32)
    proj_part = times_t(strip_input, input_down_factor)
    back_part = times_t(strip_gradient, output_weight_frozen)
    pgrad_part = times_t(strip_gradient, up_out)
    hidden_total, proj_sum, gradient_total, pgrad_sum = lax.psum(
        (h_part, proj_part, back_part, pgrad_part), "narrow"
    )
    input_rank_product = proj_sum.astype(jnp.bfloat16)
    gradient_rank_product = pgrad_sum.astype(jnp.bfloat16)
    activated_hidden, preactivation_gradient = activate(
        hidden_total,
        input_rank_product,
        gradient_total,
        gradient_rank_product,
        input_up_factor,
        output_down_factor,
    )
    act_part = times_t(activated_hidden, output_down_factor)
    pre_part = times_t(preactivation_gradient, input_up_factor)
    act_sum = lax.psum(act_part, "wide")
    pre_sum = lax.psum(pre_part, "wide")
    activation_rank_product = act_sum.astype(jnp.bfloat16)
    backward_rank_product = pre_sum.astype(jnp.bfloat16)
    input_down_gradient = adapter_scaling * transposed_product(backward_rank_product, strip_input)
    input_up_gradient = adapter_scaling * transposed_product(
        input_rank_product, preactivation_gradient
    )
    output_down_gradient = adapter_scaling * transposed_product(
        gradient_rank_product, activated_hidden
    )
    output_up_gradient = adapter_scaling * transposed_product(
        activation_rank_product, strip_gradient
    )
    reduced_total = lax.psum_scatter(
        times_t(preactivation_gradient, input_weight_frozen),
        "wide",
        scatter_dimension=0,
        tiled=True,
    )
    local_backward_part = lax.dynamic_slice_in_dim(
        backward_rank_product, lax.axis_index("wide") * tok_rows, tok_rows, 0
    )
    gradient_input_rows = (
        reduced_total
        + adapter_scaling
        * jnp.dot(local_backward_part, input_down_factor, preferred_element_type=jnp.float32)
    ).astype(jnp.bfloat16)
    return (
        gradient_input_rows,
        input_down_gradient,
        input_up_gradient,
        output_down_gradient,
        output_up_gradient,
    )


def solution(mesh):
    placed = (
        P("wide", "narrow"),
        P("wide", "narrow"),
        P("narrow", "wide"),
        P("wide", "narrow"),
        P(None, "narrow"),
        P(None, "wide"),
        P(None, "wide"),
        P(None, "narrow"),
    )
    return jax.shard_map(
        shards,
        mesh=mesh,
        in_specs=placed,
        out_specs=(
            P("wide", "narrow"),
            P(None, "narrow"),
            P(None, "wide"),
            P(None, "wide"),
            P(None, "narrow"),
        ),
        check_vma=False,
    )
```

profile of v0, /device:TPU:128, one launch (start us, length us, event | category | flops | bytes accessed | tf_op | source)
XLA Modules:
  0.0 895.6 jit_solution(6413366408804925146)
XLA Ops:
  7.2 0.0 all-reduce.7.cloned.1.call-start
  7.2 192.4 %all_gather.6 = bf16[512,768]{1,0:T(8,128)(2,1)S(1)} all-gather(bf16[8,768]{1,0:T(8,128)(2,1)} %param.9), channel_id=1, replica_groups=mesh['wide'=64,'narrow'=8] {'wide'}, dimensions={0}, use_global_device_ids=true | all-gather | bytes 798720 | tf_op jit(solution)/shard_map/all_gather | solution.py:70
  199.6 183.4 %all_gather.7 = bf16[512,768]{1,0:T(8,128)(2,1)S(1)} all-gather(bf16[8,768]{1,0:T(8,128)(2,1)} %param.8), channel_id=1, replica_groups=mesh['wide'=64,'narrow'=8] {'wide'}, dimensions={0}, use_global_device_ids=true | all-gather | bytes 798720 | tf_op jit(solution)/shard_map/all_gather | solution.py:69
  383.0 1.5 fusion.18
  384.5 1.5 fusion.20
  386.0 0.0 reduce-scatter.2.cloned.1.call-start
  386.1 0.3 fusion.21
  386.4 0.4 copy-done.4
  386.9 0.4 fusion.19
  387.2 50.7 %all-reduce.8 = (bf16[512,64]{0,1:T(8,128)(2,1)S(1)}, bf16[512,64]{0,1:T(8,128)(2,1)S(1)}) all-reduce(f32[512,64]{0,1:T(8,128)S(1)} %fusion.21, f32[512,64]{0,1:T(8,128)S(1)} %fusion.19), channel_id=1, replica_groups=mesh['wide'=64,'narrow'=8] {'narrow'}, use_global_device_ids=true, to_apply=%region_3.0 | all-reduce | flops 65536 | bytes 393216 | tf_op jit(solution)/shard_map/psum | solution.py:76
  438.0 63.3 %all-reduce.7.cloned.1.call-done = (f32[512,384]{1,0:T(8,128)}, f32[512,384]{1,0:T(8,128)}) async-done(((f32[512,384]{1,0:T(8,128)}, f32[512,384]{1,0:T(8,128)}), (f32[512,384]{1,0:T(8,128)}, f32[512,384]{1,0:T(8,128)})) %all-reduce.7.cloned.1.call-update) | async-done | bytes 1572880 | tf_op jit(solution)/shard_map/psum | solution.py:76
  501.3 1.7 multiply_convert_fusion
  503.0 0.7 fusion.3
  503.7 1.7 fusion.22
  505.5 0.0 reduce-scatter.2.cloned.1.call-update
  505.5 0.2 fusion.23
  505.7 0.2 fusion.24
  506.0 371.7 %all-reduce.9 = (bf16[512,64]{0,1:T(8,128)(2,1)S(1)}, bf16[512,64]{1,0:T(8,128)(2,1)}) all-reduce(f32[512,64]{0,1:T(8,128)S(1)} %fusion.23, f32[512,64]{1,0:T(8,128)S(1)} %fusion.24), channel_id=1, replica_groups=mesh['wide'=64,'narrow'=8] {'wide'}, use_global_device_ids=true, to_apply=%region_5.0 | all-reduce | flops 65536 | bytes 393216 | tf_op jit(solution)/shard_map/psum | solution.py:92
  877.6 1.7 convolution_multiply_fusion.5
  879.4 1.7 convolution_multiply_fusion.4
  881.0 0.9 convolution_multiply_fusion.3
  882.0 1.0 convolution_multiply_fusion.2
  883.0 4.2 reduce-scatter.2.cloned.1.call-done
  887.2 1.6 fusion.5
  (20 shorter events, 0.1 us)
Async XLA Ops:
  7.2 377.3 %copy-start = (bf16[768,384]{1,0:T(8,128)(2,1)S(1)}, bf16[768,384]{1,0:T(8,128)(2,1)}, u32[]{:S(2)}) copy-start(bf16[768,384]{1,0:T(8,128)(2,1)} %param.10) | copy-start | bytes 1769476
  7.2 375.9 %copy-start.1 = (bf16[384,768]{1,0:T(8,128)(2,1)S(1)}, bf16[384,768]{1,0:T(8,128)(2,1)}, u32[]{:S(2)}) copy-start(bf16[384,768]{1,0:T(8,128)(2,1)} %param.11) | copy-start | bytes 1769476
  7.2 494.1 %all-reduce.7.cloned.1.call-start = ((), (), s32[]{:S(2)}) async-start(), calls=%async_computation.2 | async-start | bytes 3145728 | tf_op jit(solution)/shard_map/psum | solution.py:76
  384.5 1.5 copy-start.2
  386.0 0.9 copy-start.4
  386.0 115.3 %copy-start.7 = (bf16[64,384]{1,0:T(8,128)(2,1)S(1)}, bf16[64,384]{1,0:T(8,128)(2,1)}, u32[]{:S(2)}) copy-start(bf16[64,384]{1,0:T(8,128)(2,1)} %param.13) | copy-start | bytes 147460
  386.0 501.2 %reduce-scatter.2.cloned.1.call-start = ((), (), s32[]{:S(2)}) async-start(), calls=%async_computation.1 | async-start | bytes 1597440 | tf_op jit(solution)/shard_map/reduce_scatter | solution.py:105
  387.2 115.8 %copy-start.8 = (bf16[64,384]{1,0:T(8,128)(2,1)S(1)}, bf16[64,384]{1,0:T(8,128)(2,1)}, u32[]{:S(2)}) copy-start(bf16[64,384]{1,0:T(8,128)(2,1)} %param.14) | copy-start | bytes 147460
  438.0 65.0 %copy-start.6 = (bf16[512,64]{0,1:T(8,128)(2,1)}, bf16[512,64]{0,1:T(8,128)(2,1)S(1)}, u32[]{:S(2)}) copy-start(bf16[512,64]{0,1:T(8,128)(2,1)S(1)} %get-tuple-element.7) | copy-start | bytes 196612
  438.0 65.7 %copy-start.5 = (bf16[512,64]{0,1:T(8,128)(2,1)}, bf16[512,64]{0,1:T(8,128)(2,1)S(1)}, u32[]{:S(2)}) copy-start(bf16[512,64]{0,1:T(8,128)(2,1)S(1)} %get-tuple-element.8) | copy-start | bytes 196612
  501.3 1.7 copy-start.9
  877.6 4.3 copy-start.3
Sparse Core Ops, SparseCore 0:
  386.1 115.1 all-reduce.6
  505.6 381.5 reduce-scatter.1
where the time goes:
time: 896 us
  blocking collectives  798 us (89%)
  waiting for transfers between devices  67.5 us (8%)
  matrix products  15.1 us (2%)
  between operations  14.2 us (2%)
    psum x1, blocking collectives, shards(): pre_sum = lax.psum(pre_part, 'wide')  372 us
    all_gather x1, blocking collectives, shards(): lax.all_gather(upstream_output_gradient, 'wide', axis=0, tiled=True)  192 us
    all_gather x1, blocking collectives, shards(): lax.all_gather(inputs, 'wide', axis=0, tiled=True)  183 us
    psum x1, waiting for transfers between devices, shards(): lax.psum((h_part, proj_part, back_part, pgrad_part), 'narrow')  63.3 us
    psum x1, blocking collectives, shards(): lax.psum((h_part, proj_part, back_part, pgrad_part), 'narrow')  50.7 us
  transfers between devices with their start and end apart: 2, of which 2 were waited for; matrix products, arithmetic and copies ran while one was open for 1% of the time, Pallas kernels for 0%

commit v1 on v0

v1 whole, which is shorter than its diff:
```python
import functools
import math

import jax
import jax.numpy as jnp
from jax import lax
from jax.experimental import pallas as pl
from jax.experimental.pallas import tpu as pltpu
from jax.sharding import PartitionSpec as P

MESH = pl.DeviceIdType.MESH
F32 = jnp.float32
BF16 = jnp.bfloat16
scaling = 2.0
coef = math.sqrt(2.0 / math.pi)

FAMILIES = (
    "gz", "ga", "gb", "gc", "gd", "core", "rz", "pz", "pc", "fx", "fy", "fz", "nz", "nc",
    "ec", "ez", "eg", "eh", "ya", "xa", "xb", "yb", "cz", "spare",
)
FAMILY = {name: i for i, name in enumerate(FAMILIES)}


def nn(left, right):
    return lax.dot_general(left, right, (((1,), (0,)), ((), ())), preferred_element_type=F32)


def nt(left, right):
    return lax.dot_general(left, right, (((1,), (1,)), ((), ())), preferred_element_type=F32)


def tn(left, right):
    return lax.dot_general(left, right, (((0,), (0,)), ((), ())), preferred_element_type=F32)


def kernel(
    x_ref, g_ref, w1_hbm, w2_hbm, din_ref, upin_ref, dout_ref, upout_ref,
    dx_ref, gdin_ref, gupin_ref, gdout_ref, gupout_ref,
    w1, w2, zbuf, strip, part_out, part_in, part_own, red_out, red_in,
    pre, proj, fxb, fyb, fzb, eown, ein, ezout, ezin, egb,
    dxp, c1in, c2out, c2in, czout, czin,
    wsem, ssem, rsem,
):
    w = lax.axis_index("wide")
    n = lax.axis_index("narrow")
    y, z, x = w // 16, (w // 4) % 4, w % 4
    zh, c = n // 2, n % 2
    oc = 1 - c

    def at_x(d):
        return (y * 16 + z * 4 + (x + d) % 4, n)

    def at_y(d):
        return (((y + d) % 4) * 16 + z * 4 + x, n)

    def at_z(d):
        return (y * 16 + ((z + d) % 4) * 4 + x, n)

    def at_h(d):
        return (w, ((zh + d) % 4) * 2 + c)

    other = (w, zh * 2 + oc)
    sent = []

    def push(family, slot, src, dst, to):
        i = FAMILY[family]
        copy = pltpu.make_async_remote_copy(
            src_ref=src, dst_ref=dst, send_sem=ssem.at[i, slot], recv_sem=rsem.at[i, slot],
            device_id=to, device_id_type=MESH,
        )
        copy.start()
        sent.append(copy)
        return copy

    load1 = pltpu.make_async_copy(w1_hbm, w1, wsem.at[0])
    load2 = pltpu.make_async_copy(w2_hbm, w2, wsem.at[1])
    load1.start()
    load2.start()

    barrier = pltpu.get_barrier_semaphore()
    for d in (1, 2, 3):
        for at in (at_x, at_y, at_z, at_h):
            pl.semaphore_signal(barrier, inc=1, device_id=at(d), device_id_type=MESH)
    pl.semaphore_signal(barrier, inc=1, device_id=other, device_id_type=MESH)

    zbuf[z] = jnp.concatenate([x_ref[...].astype(F32), g_ref[...].astype(F32)], 0).astype(BF16)
    pl.semaphore_wait(barrier, 13)

    copies = [push("gz", d, zbuf.at[z], zbuf.at[z], at_z(d)) for d in (2, 1, 3)]
    for copy in copies:
        copy.wait_recv()
    planes = [zbuf[i].astype(F32) for i in range(4)]
    for t in range(2):
        rows = slice(8 * t, 8 * t + 8)
        strip[0, y, t, x] = jnp.concatenate([planes[0][rows], planes[1][rows]], 0).astype(BF16)
        strip[1, x, t, y] = jnp.concatenate([planes[2][rows], planes[3][rows]], 0).astype(BF16)
    copies = []
    for d in (2, 1, 3):
        mine = strip.at[0, y, :, x]
        copies.append(push("ga", d, mine, mine, at_x(d)))
        mine = strip.at[1, x, :, y]
        copies.append(push("gb", d, mine, mine, at_y(d)))
    for copy in copies:
        copy.wait_recv()
    copies = []
    for d in (2, 1, 3):
        mine = strip.at[0, y]
        copies.append(push("gc", d, mine, mine, at_y(d)))
        mine = strip.at[1, x]
        copies.append(push("gd", d, mine, mine, at_x(d)))
    load1.wait()
    load2.wait()
    for copy in copies:
        copy.wait_recv()

    def partial(half, store):
        xs = strip[half, :, 0].reshape(256, 768)
        gs = strip[half, :, 1].reshape(256, 768)
        store(0, 384, nn(xs, w1[...]))
        store(384, 384, nt(gs, w2[...]))
        store(768, 64, nt(xs, din_ref[...]))
        store(832, 64, nt(gs, upout_ref[...]))

    def store_out(start, size, value):
        part_out[:, :, start:start + size] = value.astype(BF16).reshape(4, 64, size)

    def store_own(start, size, value):
        part_own[:, :, start:start + size] = value.reshape(4, 64, size)

    partial(oc, store_out)
    copy = push("core", 0, part_out, part_in, other)
    partial(c, store_own)
    copy.wait_recv()
    copies = []
    for d in (2, 1, 3):
        k = (zh + d) % 4
        red_out[d] = (part_own[k] + part_in[k].astype(F32)).astype(BF16)
        copies.append(push("rz", d, red_out.at[d], red_in.at[d], at_h(d)))
    total = part_own[zh] + part_in[zh].astype(F32)
    for copy in copies:
        copy.wait_recv()
    for d in (1, 2, 3):
        total = total + red_in[d].astype(F32)

    proj_in = total[:, 768:832].astype(BF16)
    proj_grad = total[:, 832:896].astype(BF16)
    v = total[:, :384] + scaling * nn(proj_in, upin_ref[...])
    grad = total[:, 384:768] + scaling * nn(proj_grad, dout_ref[...])
    t = jnp.tanh(coef * (v + 0.044715 * v * v * v))
    act = (0.5 * v * (1.0 + t)).astype(BF16)
    slope = 0.5 * (1.0 + t) + 0.5 * v * (1.0 - t * t) * coef * (1.0 + 3.0 * 0.044715 * v * v)
    pre_own = (grad * slope).astype(BF16)

    pre[c, zh] = pre_own
    mine = pre.at[c, zh]
    pz = {d: push("pz", d, mine, mine, at_h(d)) for d in (2, 1, 3)}
    pc = [push("pc", 0, mine, mine, other)]

    fxb[x] = jnp.concatenate([nt(act, dout_ref[...]), nt(pre_own, upin_ref[...])], 1)
    fx = [push("fx", d, fxb.at[x], fxb.at[x], at_x(d)) for d in (2, 1, 3)]
    eown[0] = scaling * tn(proj_in, pre_own)
    eown[1] = scaling * tn(proj_grad, act)
    ec = push("ec", 0, eown.at[oc], ein, other)

    for copy in fx:
        copy.wait_recv()
    fyb[y] = fxb[0] + fxb[1] + fxb[2] + fxb[3]
    fy = [push("fy", d, fyb.at[y], fyb.at[y], at_y(d)) for d in (2, 1, 3)]

    ec.wait_recv()
    esum = eown[c] + ein[...]
    ezout[...] = esum.astype(BF16).reshape(4, 16, 384)
    ez = [push("ez", d, ezout.at[(zh + d) % 4], ezin.at[d], at_h(d)) for d in (2, 1, 3)]

    for copy in fy:
        copy.wait_recv()
    fzb[z] = fyb[0] + fyb[1] + fyb[2] + fyb[3]
    fz = [push("fz", d, fzb.at[z], fzb.at[z], at_z(d)) for d in (2, 1, 3)]

    for d in (1, 3, 2):
        pz[d].wait_recv()
        got = pre.at[c, (zh + 4 - d) % 4]
        pc.append(push("pc", d, got, got, other))

    for copy in fz:
        copy.wait_recv()
    proj[c, zh] = (fzb[0] + fzb[1] + fzb[2] + fzb[3]).astype(BF16)
    mine = proj.at[c, zh]
    nz = {d: push("nz", d, mine, mine, at_h(d)) for d in (2, 1, 3)}
    nc = [push("nc", 0, mine, mine, other)]

    for copy in pc:
        copy.wait_recv()
    for h in range(2):
        rows = pre[h].reshape(256, 384)
        dxp[h] = nt(rows, w1[...]).astype(BF16).reshape(4, 4, 16, 768)
    c1 = []
    for d in (2, 1, 3):
        c1.append(push("ya", d, dxp.at[0, (y + d) % 4], c1in.at[0, d], at_y(d)))
        c1.append(push("xb", d, dxp.at[1, (x + d) % 4], c1in.at[1, d], at_x(d)))

    for copy in ez:
        copy.wait_recv()
    esl = ezout[zh].astype(F32)
    for d in (1, 2, 3):
        esl = esl + ezin[d].astype(F32)
    egb[c, zh] = esl.astype(BF16)
    mine = egb.at[c, zh]
    eg = {d: push("eg", d, mine, mine, at_h(d)) for d in (2, 1, 3)}
    eh = [push("eh", 0, mine, mine, other)]

    for copy in c1:
        copy.wait_recv()
    c2 = []
    s0 = dxp[0, y].astype(F32)
    s1 = dxp[1, x].astype(F32)
    for d in (1, 2, 3):
        s0 = s0 + c1in[0, d].astype(F32)
        s1 = s1 + c1in[1, d].astype(F32)
    c2out[0] = s0.astype(BF16)
    c2out[1] = s1.astype(BF16)
    for d in (2, 1, 3):
        c2.append(push("xa", d, c2out.at[0, (x + d) % 4], c2in.at[0, d], at_x(d)))
        c2.append(push("yb", d, c2out.at[1, (y + d) % 4], c2in.at[1, d], at_y(d)))

    for d in (1, 3, 2):
        nz[d].wait_recv()
        got = proj.at[c, (zh + 4 - d) % 4]
        nc.append(push("nc", d, got, got, other))

    for copy in c2:
        copy.wait_recv()
    s0 = c2out[0, x].astype(F32)
    s1 = c2out[1, y].astype(F32)
    for d in (1, 2, 3):
        s0 = s0 + c2in[0, d].astype(F32)
        s1 = s1 + c2in[1, d].astype(F32)
    czout[0] = s0[:8]
    czout[1] = s0[8:]
    czout[2] = s1[:8]
    czout[3] = s1[8:]
    cz = [push("cz", d, czout.at[(z + d) % 4], czin.at[d], at_z(d)) for d in (2, 1, 3)]

    for d in (1, 3, 2):
        eg[d].wait_recv()
        got = egb.at[c, (zh + 4 - d) % 4]
        eh.append(push("eh", d, got, got, other))

    for copy in nc:
        copy.wait_recv()
    rank = proj[...].reshape(512, 128)
    xs = strip[:, :, 0].reshape(512, 768)
    gs = strip[:, :, 1].reshape(512, 768)
    gupout_ref[...] = scaling * tn(rank[:, :64], gs)
    gdin_ref[...] = scaling * tn(rank[:, 64:], xs)

    for copy in eh:
        copy.wait_recv()
    gupin_ref[...] = egb[0].reshape(64, 384).astype(F32)
    gdout_ref[...] = egb[1].reshape(64, 384).astype(F32)

    half = z // 2
    k = jnp.where(half == 0, y, x)
    j = jnp.where(half == 0, x, y)
    rows = proj[half, k, pl.ds(pl.multiple_of(j * 16, 16), 16), :].astype(F32)
    back = jnp.where(z % 2 == 0, rows[:8], rows[8:])[:, 64:].astype(BF16)
    extra = scaling * nn(back, din_ref[...])
    for copy in cz:
        copy.wait_recv()
    out = czout[z] + extra
    for d in (1, 2, 3):
        out = out + czin[d]
    dx_ref[...] = out.astype(BF16)

    for copy in sent:
        copy.wait_send()


def shards(x, g, w1, w2, din, upin, dout, upout):
    vmem = pl.BlockSpec(memory_space=pltpu.VMEM)
    hbm = pl.BlockSpec(memory_space=pl.ANY)
    nf = len(FAMILIES)
    return pl.pallas_call(
        kernel,
        out_shape=(
            jax.ShapeDtypeStruct((8, 768), BF16),
            jax.ShapeDtypeStruct((64, 768), F32),
            jax.ShapeDtypeStruct((64, 384), F32),
            jax.ShapeDtypeStruct((64, 384), F32),
            jax.ShapeDtypeStruct((64, 768), F32),
        ),
        in_specs=[vmem, vmem, hbm, hbm, vmem, vmem, vmem, vmem],
        out_specs=(vmem,) * 5,
        scratch_shapes=[
            pltpu.VMEM((768, 384), BF16),
            pltpu.VMEM((384, 768), BF16),
            pltpu.VMEM((4, 16, 768), BF16),
            pltpu.VMEM((2, 4, 2, 4, 16, 768), BF16),
            pltpu.VMEM((4, 64, 896), BF16),
            pltpu.VMEM((4, 64, 896), BF16),
            pltpu.VMEM((4, 64, 896), F32),
            pltpu.VMEM((4, 64, 896), BF16),
            pltpu.VMEM((4, 64, 896), BF16),
            pltpu.VMEM((2, 4, 64, 384), BF16),
            pltpu.VMEM((2, 4, 64, 128), BF16),
            pltpu.VMEM((4, 64, 128), F32),
            pltpu.VMEM((4, 64, 128), F32),
            pltpu.VMEM((4, 64, 128), F32),
            pltpu.VMEM((2, 64, 384), F32),
            pltpu.VMEM((64, 384), F32),
            pltpu.VMEM((4, 16, 384), BF16),
            pltpu.VMEM((4, 16, 384), BF16),
            pltpu.VMEM((2, 4, 16, 384), BF16),
            pltpu.VMEM((2, 4, 4, 16, 768), BF16),
            pltpu.VMEM((2, 4, 4, 16, 768), BF16),
            pltpu.VMEM((2, 4, 16, 768), BF16),
            pltpu.VMEM((2, 4, 16, 768), BF16),
            pltpu.VMEM((4, 8, 768), F32),
            pltpu.VMEM((4, 8, 768), F32),
            pltpu.SemaphoreType.DMA((2,)),
            pltpu.SemaphoreType.DMA((nf, 4)),
            pltpu.SemaphoreType.DMA((nf, 4)),
        ],
        compiler_params=pltpu.CompilerParams(
            collective_id=0, has_side_effects=True, vmem_limit_bytes=48 * 1024 * 1024
        ),
    )(x, g, w1, w2, din, upin, dout, upout)


def solution(mesh):
    return jax.shard_map(
        shards,
        mesh=mesh,
        in_specs=(
            P("wide", "narrow"),
            P("wide", "narrow"),
            P("narrow", "wide"),
            P("wide", "narrow"),
            P(None, "narrow"),
            P(None, "wide"),
            P(None, "wide"),
            P(None, "narrow"),
        ),
        out_specs=(
            P("wide", "narrow"),
            P(None, "narrow"),
            P(None, "wide"),
            P(None, "wide"),
            P(None, "narrow"),
        ),
        check_vma=False,
    )
```

time: 896 us -> 103 us (0.11)
  the two profiles are of different devices: /device:TPU:128 before, /device:TPU:1 now
where the time goes in v1:
time: 103 us
  Pallas kernels  91.9 us (89%)
  local copies, waits for them, and re-layouts  10.1 us (10%)
    pallas_call x1, Pallas kernels, shards(): pl.pallas_call(kernel, out_shape=(jax.ShapeDtypeStruct((8, 768), BF16), j...  91.9 us
    unnamed x21, local copies, waits for them, and re-layouts  10.1 us

profile of v1, /device:TPU:1, one launch (start us, length us, event | category | flops | bytes accessed | tf_op | source)
XLA Modules:
  0.0 102.8 jit_solution(258996641960569151)
XLA Ops:
  0.6 0.0 copy-start
  0.6 1.1 %copy-done = bf16[768,384]{1,0:T(8,128)(2,1)S(1)} copy-done((bf16[768,384]{1,0:T(8,128)(2,1)S(1)}, bf16[768,384]{1,0:T(8,128)(2,1)}, u32[]{:S(2)}) %copy-start) | copy-done | bytes 589848
  1.7 0.0 copy-start.1
  1.7 1.1 %copy-done.1 = bf16[384,768]{1,0:T(8,128)(2,1)S(1)} copy-done((bf16[384,768]{1,0:T(8,128)(2,1)S(1)}, bf16[384,768]{1,0:T(8,128)(2,1)}, u32[]{:S(2)}) %copy-start.1) | copy-done | bytes 589848
  2.8 0.0 copy-start.2
  2.8 0.9 copy-done.2
  3.7 0.0 copy-start.3
  3.7 0.9 copy-done.3
  4.6 0.0 copy-start.4
  4.6 0.8 copy-done.4
  5.3 0.0 copy-start.5
  5.4 0.8 copy-done.5
  6.1 0.0 copy-start.6
  6.2 0.7 copy-done.6
  6.9 0.0 copy-start.7
  6.9 0.7 copy-done.7
  7.6 91.9 %shard_map.119 = (bf16[8,768]{1,0:T(8,128)(2,1)S(1)}, f32[64,768]{1,0:T(8,128)S(1)}, f32[64,384]{1,0:T(8,128)S(1)}, f32[64,384]{1,0:T(8,128)S(1)}, f32[64,768]{1,0:T(8,128)S(1)}) custom-call(bf16[8,768]{1,0:T(8,128)(2,1)S(1)} %copy-done.6, bf16[8,768]{1,0:T(8,128)(2,1)S(1)} %copy-done.7, bf16[768,384]{1,0:T(8,128)(2,1)S(1)} %copy-done, ...), custom_call_target="tpu_custom_call" | custom-call | tf_op jit(solution)/shard_map/pallas_call | solution.py:283
  99.5 0.6 copy.18
  100.1 0.7 copy.19
  100.8 0.6 copy.20
  101.4 0.6 copy.21
  102.1 0.7 copy.22
Async XLA Ops:
  0.6 1.1 %copy-start = (bf16[768,384]{1,0:T(8,128)(2,1)S(1)}, bf16[768,384]{1,0:T(8,128)(2,1)}, u32[]{:S(2)}) copy-start(bf16[768,384]{1,0:T(8,128)(2,1)} %w1_hbm.1) | copy-start | bytes 1769476
  1.7 1.1 %copy-start.1 = (bf16[384,768]{1,0:T(8,128)(2,1)S(1)}, bf16[384,768]{1,0:T(8,128)(2,1)}, u32[]{:S(2)}) copy-start(bf16[384,768]{1,0:T(8,128)(2,1)} %w2_hbm.1) | copy-start | bytes 1769476
  2.8 0.9 copy-start.2
  3.7 0.9 copy-start.3
  4.6 0.8 copy-start.4
  5.3 0.8 copy-start.5
  6.1 0.7 copy-start.6
  6.9 0.7 copy-start.7

commit v2 on v1

--- a/solution.py
+++ b/solution.py
@@ -34,9 +34,9 @@
 
 
 def kernel(
-    x_ref, g_ref, w1_hbm, w2_hbm, din_ref, upin_ref, dout_ref, upout_ref,
+    x_hbm, g_hbm, w1_hbm, w2_hbm, din_hbm, upin_hbm, dout_hbm, upout_hbm,
     dx_ref, gdin_ref, gupin_ref, gdout_ref, gupout_ref,
-    w1, w2, zbuf, strip, part_out, part_in, part_own, red_out, red_in,
+    x_ref, g_ref, w1, w2, din_ref, upin_ref, dout_ref, upout_ref, zbuf, strip, part_out, part_in, part_own, red_out, red_in,
     pre, proj, fxb, fyb, fzb, eown, ein, ezout, ezin, egb,
     dxp, c1in, c2out, c2in, czout, czin,
     wsem, ssem, rsem,
@@ -72,10 +72,15 @@
         sent.append(copy)
         return copy
 
-    load1 = pltpu.make_async_copy(w1_hbm, w1, wsem.at[0])
-    load2 = pltpu.make_async_copy(w2_hbm, w2, wsem.at[1])
-    load1.start()
-    load2.start()
+    loads = [
+        pltpu.make_async_copy(src, dst, wsem.at[i])
+        for i, (src, dst) in enumerate((
+            (x_hbm, x_ref), (g_hbm, g_ref), (w1_hbm, w1), (w2_hbm, w2), (din_hbm, din_ref),
+            (upin_hbm, upin_ref), (dout_hbm, dout_ref), (upout_hbm, upout_ref),
+        ))
+    ]
+    for load in loads:
+        load.start()
 
     barrier = pltpu.get_barrier_semaphore()
     for d in (1, 2, 3):
@@ -83,6 +88,8 @@
             pl.semaphore_signal(barrier, inc=1, device_id=at(d), device_id_type=MESH)
     pl.semaphore_signal(barrier, inc=1, device_id=other, device_id_type=MESH)
 
+    loads[0].wait()
+    loads[1].wait()
     zbuf[z] = jnp.concatenate([x_ref[...].astype(F32), g_ref[...].astype(F32)], 0).astype(BF16)
     pl.semaphore_wait(barrier, 13)
 
@@ -108,8 +115,8 @@
         copies.append(push("gc", d, mine, mine, at_y(d)))
         mine = strip.at[1, x]
         copies.append(push("gd", d, mine, mine, at_x(d)))
-    load1.wait()
-    load2.wait()
+    for load in loads[2:]:
+        load.wait()
     for copy in copies:
         copy.wait_recv()
 
@@ -122,7 +129,7 @@
         store(832, 64, nt(gs, upout_ref[...]))
 
     def store_out(start, size, value):
-        part_out[:, :, start:start + size] = value.astype(BF16).reshape(4, 64, size)
+        part_out[:, :, start:start + size] = value.reshape(4, 64, size)
 
     def store_own(start, size, value):
         part_own[:, :, start:start + size] = value.reshape(4, 64, size)
@@ -134,9 +141,9 @@
     copies = []
     for d in (2, 1, 3):
         k = (zh + d) % 4
-        red_out[d] = (part_own[k] + part_in[k].astype(F32)).astype(BF16)
+        red_out[d] = (part_own[k] + part_in[k]).astype(BF16)
         copies.append(push("rz", d, red_out.at[d], red_in.at[d], at_h(d)))
-    total = part_own[zh] + part_in[zh].astype(F32)
+    total = part_own[zh] + part_in[zh]
     for copy in copies:
         copy.wait_recv()
     for d in (1, 2, 3):
@@ -217,8 +224,8 @@
     for d in (1, 2, 3):
         s0 = s0 + c1in[0, d].astype(F32)
         s1 = s1 + c1in[1, d].astype(F32)
-    c2out[0] = s0.astype(BF16)
-    c2out[1] = s1.astype(BF16)
+    c2out[0] = s0
+    c2out[1] = s1
     for d in (2, 1, 3):
         c2.append(push("xa", d, c2out.at[0, (x + d) % 4], c2in.at[0, d], at_x(d)))
         c2.append(push("yb", d, c2out.at[1, (y + d) % 4], c2in.at[1, d], at_y(d)))
@@ -230,11 +237,11 @@
 
     for copy in c2:
         copy.wait_recv()
-    s0 = c2out[0, x].astype(F32)
-    s1 = c2out[1, y].astype(F32)
-    for d in (1, 2, 3):
-        s0 = s0 + c2in[0, d].astype(F32)
-        s1 = s1 + c2in[1, d].astype(F32)
+    s0 = c2out[0, x]
+    s1 = c2out[1, y]
+    for d in (1, 2, 3):
+        s0 = s0 + c2in[0, d]
+        s1 = s1 + c2in[1, d]
     czout[0] = s0[:8]
     czout[1] = s0[8:]
     czout[2] = s1[:8]
@@ -276,28 +283,44 @@
         copy.wait_send()
 
 
+def hand_over(*refs):
+    sems = refs[10]
+    copies = [pltpu.make_async_copy(refs[i], refs[5 + i], sems.at[i]) for i in range(5)]
+    for copy in copies:
+        copy.start()
+    for copy in copies:
+        copy.wait()
+
+
 def shards(x, g, w1, w2, din, upin, dout, upout):
     vmem = pl.BlockSpec(memory_space=pltpu.VMEM)
     hbm = pl.BlockSpec(memory_space=pl.ANY)
     nf = len(FAMILIES)
-    return pl.pallas_call(
+    shapes = (
+        jax.ShapeDtypeStruct((8, 768), BF16),
+        jax.ShapeDtypeStruct((64, 768), F32),
+        jax.ShapeDtypeStruct((64, 384), F32),
+        jax.ShapeDtypeStruct((64, 384), F32),
+        jax.ShapeDtypeStruct((64, 768), F32),
+    )
+    made = pl.pallas_call(
         kernel,
-        out_shape=(
-            jax.ShapeDtypeStruct((8, 768), BF16),
-            jax.ShapeDtypeStruct((64, 768), F32),
-            jax.ShapeDtypeStruct((64, 384), F32),
-            jax.ShapeDtypeStruct((64, 384), F32),
-            jax.ShapeDtypeStruct((64, 768), F32),
-        ),
-        in_specs=[vmem, vmem, hbm, hbm, vmem, vmem, vmem, vmem],
+        out_shape=shapes,
+        in_specs=[hbm] * 8,
         out_specs=(vmem,) * 5,
         scratch_shapes=[
+            pltpu.VMEM((8, 768), BF16),
+            pltpu.VMEM((8, 768), BF16),
             pltpu.VMEM((768, 384), BF16),
             pltpu.VMEM((384, 768), BF16),
+            pltpu.VMEM((64, 768), BF16),
+            pltpu.VMEM((64, 384), BF16),
+            pltpu.VMEM((64, 384), BF16),
+            pltpu.VMEM((64, 768), BF16),
             pltpu.VMEM((4, 16, 768), BF16),
             pltpu.VMEM((2, 4, 2, 4, 16, 768), BF16),
-            pltpu.VMEM((4, 64, 896), BF16),
-            pltpu.VMEM((4, 64, 896), BF16),
+            pltpu.VMEM((4, 64, 896), F32),
+            pltpu.VMEM((4, 64, 896), F32),
             pltpu.VMEM((4, 64, 896), F32),
             pltpu.VMEM((4, 64, 896), BF16),
             pltpu.VMEM((4, 64, 896), BF16),
@@ -313,18 +336,26 @@
             pltpu.VMEM((2, 4, 16, 384), BF16),
             pltpu.VMEM((2, 4, 4, 16, 768), BF16),
             pltpu.VMEM((2, 4, 4, 16, 768), BF16),
-            pltpu.VMEM((2, 4, 16, 768), BF16),
-            pltpu.VMEM((2, 4, 16, 768), BF16),
+            pltpu.VMEM((2, 4, 16, 768), F32),
+            pltpu.VMEM((2, 4, 16, 768), F32),
             pltpu.VMEM((4, 8, 768), F32),
             pltpu.VMEM((4, 8, 768), F32),
-            pltpu.SemaphoreType.DMA((2,)),
+            pltpu.SemaphoreType.DMA((8,)),
             pltpu.SemaphoreType.DMA((nf, 4)),
             pltpu.SemaphoreType.DMA((nf, 4)),
         ],
         compiler_params=pltpu.CompilerParams(
-            collective_id=0, has_side_effects=True, vmem_limit_bytes=48 * 1024 * 1024
+            collective_id=0, has_side_effects=True, vmem_limit_bytes=60 * 1024 * 1024
         ),
     )(x, g, w1, w2, din, upin, dout, upout)
+    return pl.pallas_call(
+        hand_over,
+        out_shape=shapes,
+        in_specs=[hbm] * 5,
+        out_specs=(hbm,) * 5,
+        scratch_shapes=[pltpu.SemaphoreType.DMA((5,))],
+        compiler_params=pltpu.CompilerParams(vmem_limit_bytes=60 * 1024 * 1024),
+    )(*made)
 
 
 def solution(mesh):

time: 103 us -> 113 us (1.097)
  Pallas kernels: 91.9 us -> 112 us
  local copies, waits for them, and re-layouts: 10.1 us -> 0 us
    pallas_call x1 -> x2, Pallas kernels: 91.9 us -> 112 us  [the longest x1 92.6 us: shards(): pl.pallas_call(kernel, out_shape=shapes, in_specs=[hbm] * 8, out_specs=(v...]
    unnamed x21 -> x0, local copies, waits for them, and re-layouts: 10.1 us -> none
where the time goes in v2:
time: 113 us
  Pallas kernels  112 us (99%)
    pallas_call x1, Pallas kernels, shards(): pl.pallas_call(kernel, out_shape=shapes, in_specs=[hbm] * 8, out_specs=(v...  92.6 us
    pallas_call x1, Pallas kernels, shards(): pl.pallas_call(hand_over, out_shape=shapes, in_specs=[hbm] * 5, out_specs...  19.4 us

profile of v2, /device:TPU:1, one launch (start us, length us, event | category | flops | bytes accessed | tf_op | source)
XLA Modules:
  0.0 112.7 jit_solution(2104218986272879878)
XLA Ops:
  0.6 92.6 %shard_map.119 = (bf16[8,768]{1,0:T(8,128)(2,1)}, f32[64,768]{1,0:T(8,128)}, f32[64,384]{1,0:T(8,128)}, f32[64,384]{1,0:T(8,128)}, f32[64,768]{1,0:T(8,128)}) custom-call(bf16[8,768]{1,0:T(8,128)(2,1)} %x_hbm.1, bf16[8,768]{1,0:T(8,128)(2,1)} %g_hbm.1, bf16[768,384]{1,0:T(8,128)(2,1)} %w1_hbm.1, bf16[384,768]{1,0:T(8,128)(2,1)} %w2_hbm.1, ...), custom_call_target="tpu_custom_call" | custom-call | tf_op jit(solution)/shard_map/pallas_call | solution.py:306
  93.3 19.4 %shard_map.120 = (bf16[8,768]{1,0:T(8,128)(2,1)}, f32[64,768]{1,0:T(8,128)}, f32[64,384]{1,0:T(8,128)}, f32[64,384]{1,0:T(8,128)}, f32[64,768]{1,0:T(8,128)}) custom-call(bf16[8,768]{1,0:T(8,128)(2,1)} %get-tuple-element.10.refs_0_, f32[64,768]{1,0:T(8,128)} %get-tuple-element.11.refs_1_, f32[64,384]{1,0:T(8,128)} %get-tuple-element.12.refs_2_, ...), custom_call_target="tpu_custom_call" | custom-call | tf_op jit(solution)/shard_map/pallas_call | solution.py:351

commit v3 on v2

--- a/solution.py
+++ b/solution.py
@@ -284,11 +284,15 @@
 
 
 def hand_over(*refs):
-    sems = refs[10]
-    copies = [pltpu.make_async_copy(refs[i], refs[5 + i], sems.at[i]) for i in range(5)]
-    for copy in copies:
+    ins, outs, held, sems = refs[:5], refs[5:10], refs[10:15], refs[15]
+    reads = [pltpu.make_async_copy(ins[i], held[i], sems.at[0, i]) for i in range(5)]
+    writes = [pltpu.make_async_copy(held[i], outs[i], sems.at[1, i]) for i in range(5)]
+    for copy in reads:
         copy.start()
-    for copy in copies:
+    for read, write in zip(reads, writes):
+        read.wait()
+        write.start()
+    for copy in writes:
         copy.wait()
 
 
@@ -353,7 +357,8 @@
         out_shape=shapes,
         in_specs=[hbm] * 5,
         out_specs=(hbm,) * 5,
-        scratch_shapes=[pltpu.SemaphoreType.DMA((5,))],
+        scratch_shapes=[pltpu.VMEM(t.shape, t.dtype) for t in shapes]
+        + [pltpu.SemaphoreType.DMA((2, 5))],
         compiler_params=pltpu.CompilerParams(vmem_limit_bytes=60 * 1024 * 1024),
     )(*made)
 

time: 113 us -> 95.5 us (0.85)
  Pallas kernels: 112 us -> 94.5 us
    pallas_call x1, Pallas kernels: 19.4 us -> 1.9 us  [shards(): pl.pallas_call(hand_over, out_shape=shapes, in_specs=[hbm] * 5, out_specs...]
where the time goes in v3:
time: 95.5 us; the launch traced here: 95.2 us
  Pallas kernels  94.5 us (99%)
    pallas_call x1, Pallas kernels, shards(): pl.pallas_call(kernel, out_shape=shapes, in_specs=[hbm] * 8, out_specs=(v...  92.6 us

profile of v3, /device:TPU:1, one launch (start us, length us, event | category | flops | bytes accessed | tf_op | source)
XLA Modules:
  0.0 95.2 jit_solution(11104235402355166472)
XLA Ops:
  0.6 92.6 %shard_map.119 = (bf16[8,768]{1,0:T(8,128)(2,1)}, f32[64,768]{1,0:T(8,128)}, f32[64,384]{1,0:T(8,128)}, f32[64,384]{1,0:T(8,128)}, f32[64,768]{1,0:T(8,128)}) custom-call(bf16[8,768]{1,0:T(8,128)(2,1)} %x_hbm.1, bf16[8,768]{1,0:T(8,128)(2,1)} %g_hbm.1, bf16[768,384]{1,0:T(8,128)(2,1)} %w1_hbm.1, bf16[384,768]{1,0:T(8,128)(2,1)} %w2_hbm.1, ...), custom_call_target="tpu_custom_call" | custom-call | tf_op jit(solution)/shard_map/pallas_call | solution.py:310
  93.3 1.9 %shard_map.120 = (bf16[8,768]{1,0:T(8,128)(2,1)}, f32[64,768]{1,0:T(8,128)}, f32[64,384]{1,0:T(8,128)}, f32[64,384]{1,0:T(8,128)}, f32[64,768]{1,0:T(8,128)}) custom-call(bf16[8,768]{1,0:T(8,128)(2,1)} %get-tuple-element.10.refs_0_, f32[64,768]{1,0:T(8,128)} %get-tuple-element.11.refs_1_, f32[64,384]{1,0:T(8,128)} %get-tuple-element.12.refs_2_, ...), custom_call_target="tpu_custom_call" | custom-call | tf_op jit(solution)/shard_map/pallas_call | solution.py:355

commit v4 on v3

--- a/solution.py
+++ b/solution.py
@@ -15,10 +15,12 @@
 coef = math.sqrt(2.0 / math.pi)
 
 FAMILIES = (
-    "gz", "ga", "gb", "gc", "gd", "core", "rz", "pz", "pc", "fx", "fy", "fz", "nz", "nc",
-    "ec", "ez", "eg", "eh", "ya", "xa", "xb", "yb", "cz", "spare",
+    "gz", "ga", "gb", "gc", "gd", "core", "cj", "rz0", "rz1", "rz2", "rz3", "rj", "pj",
+    "pz0", "pz1", "pz2", "pz3", "pc0", "pc1", "pc2", "pc3", "fx", "fy", "fz", "nz", "nc",
+    "ec", "ez", "eg", "eh", "ya", "xa", "xb", "yb", "cz",
 )
 FAMILY = {name: i for i, name in enumerate(FAMILIES)}
+ORDER = (0, 1, 3, 2)
 
 
 def nn(left, right):
@@ -36,8 +38,9 @@
 def kernel(
     x_hbm, g_hbm, w1_hbm, w2_hbm, din_hbm, upin_hbm, dout_hbm, upout_hbm,
     dx_ref, gdin_ref, gupin_ref, gdout_ref, gupout_ref,
-    x_ref, g_ref, w1, w2, din_ref, upin_ref, dout_ref, upout_ref, zbuf, strip, part_out, part_in, part_own, red_out, red_in,
-    pre, proj, fxb, fyb, fzb, eown, ein, ezout, ezin, egb,
+    x_ref, g_ref, w1, w2, din_ref, upin_ref, dout_ref, upout_ref,
+    zbuf, strip, part, part_in, pj, pj_in, red_out, red_in, pj_out, pj_red, pj_all,
+    act_all, pre, proj, fxb, fyb, fzb, eown, ein, ezout, ezin, egb,
     dxp, c1in, c2out, c2in, czout, czin,
     wsem, ssem, rsem,
 ):
@@ -109,102 +112,147 @@
         copies.append(push("gb", d, mine, mine, at_y(d)))
     for copy in copies:
         copy.wait_recv()
-    copies = []
-    for d in (2, 1, 3):
+    gc, gd = {}, {}
+    for d in (1, 3, 2):
         mine = strip.at[0, y]
-        copies.append(push("gc", d, mine, mine, at_y(d)))
+        gc[d] = push("gc", d, mine, mine, at_y(d))
         mine = strip.at[1, x]
-        copies.append(push("gd", d, mine, mine, at_x(d)))
+        gd[d] = push("gd", d, mine, mine, at_x(d))
     for load in loads[2:]:
         load.wait()
-    for copy in copies:
-        copy.wait_recv()
-
-    def partial(half, store):
-        xs = strip[half, :, 0].reshape(256, 768)
-        gs = strip[half, :, 1].reshape(256, 768)
-        store(0, 384, nn(xs, w1[...]))
-        store(384, 384, nt(gs, w2[...]))
-        store(768, 64, nt(xs, din_ref[...]))
-        store(832, 64, nt(gs, upout_ref[...]))
-
-    def store_out(start, size, value):
-        part_out[:, :, start:start + size] = value.reshape(4, 64, size)
-
-    def store_own(start, size, value):
-        part_own[:, :, start:start + size] = value.reshape(4, 64, size)
-
-    partial(oc, store_out)
-    copy = push("core", 0, part_out, part_in, other)
-    partial(c, store_own)
-    copy.wait_recv()
-    copies = []
+
+    core = {}
+
+    def multiply(d):
+        if d:
+            gc[d].wait_recv()
+            gd[d].wait_recv()
+        ka, kb = (y + 4 - d) % 4, (x + 4 - d) % 4
+        xs = jnp.concatenate([strip[0, ka, 0].reshape(64, 768), strip[1, kb, 0].reshape(64, 768)], 0)
+        gs = jnp.concatenate([strip[0, ka, 1].reshape(64, 768), strip[1, kb, 1].reshape(64, 768)], 0)
+        hp = nn(xs, w1[...])
+        bp = nt(gs, w2[...])
+        for h in range(2):
+            rows = slice(64 * h, 64 * h + 64)
+            part[d, h, :, :, :384] = hp[rows].reshape(4, 16, 384)
+            part[d, h, :, :, 384:] = bp[rows].reshape(4, 16, 384)
+        core[d] = push("core", d, part.at[d, oc], part_in.at[d], other)
+        if d == 0:
+            both = jnp.concatenate([nt(xs, din_ref[...]), nt(gs, upout_ref[...])], 1)
+            pj[...] = both.reshape(2, 4, 16, 128)
+            core["j"] = push("cj", 0, pj.at[oc], pj_in, other)
+
+    rz = {}
+
+    def scatter(d):
+        core[d].wait_recv()
+        red_out[d] = (part[d, c] + part_in[d]).astype(BF16)
+        rz[d] = [
+            push("rz%d" % d, e, red_out.at[d, (zh + e) % 4], red_in.at[e, d], at_h(e))
+            for e in (2, 1, 3)
+        ]
+        if d == 0:
+            core["j"].wait_recv()
+            pj_out[...] = (pj[c] + pj_in[...]).astype(BF16)
+            rz["j"] = [
+                push("rj", e, pj_out.at[(zh + e) % 4], pj_red.at[e], at_h(e)) for e in (2, 1, 3)
+            ]
+
+    for d in ORDER:
+        multiply(d)
+        scatter(d)
+
+    for copy in rz["j"]:
+        copy.wait_recv()
+    total = pj[c, zh] + pj_in[zh]
+    for e in (1, 2, 3):
+        total = total + pj_red[e].astype(F32)
+    pj_all[0] = total.astype(BF16)
+    pjc = {}
     for d in (2, 1, 3):
-        k = (zh + d) % 4
-        red_out[d] = (part_own[k] + part_in[k]).astype(BF16)
-        copies.append(push("rz", d, red_out.at[d], red_in.at[d], at_h(d)))
-    total = part_own[zh] + part_in[zh]
-    for copy in copies:
-        copy.wait_recv()
-    for d in (1, 2, 3):
-        total = total + red_in[d].astype(F32)
-
-    proj_in = total[:, 768:832].astype(BF16)
-    proj_grad = total[:, 832:896].astype(BF16)
-    v = total[:, :384] + scaling * nn(proj_in, upin_ref[...])
-    grad = total[:, 384:768] + scaling * nn(proj_grad, dout_ref[...])
-    t = jnp.tanh(coef * (v + 0.044715 * v * v * v))
-    act = (0.5 * v * (1.0 + t)).astype(BF16)
-    slope = 0.5 * (1.0 + t) + 0.5 * v * (1.0 - t * t) * coef * (1.0 + 3.0 * 0.044715 * v * v)
-    pre_own = (grad * slope).astype(BF16)
-
-    pre[c, zh] = pre_own
-    mine = pre.at[c, zh]
-    pz = {d: push("pz", d, mine, mine, at_h(d)) for d in (2, 1, 3)}
-    pc = [push("pc", 0, mine, mine, other)]
-
-    fxb[x] = jnp.concatenate([nt(act, dout_ref[...]), nt(pre_own, upin_ref[...])], 1)
+        to = (oc * at_y(d)[0] + c * at_x(d)[0], n)
+        pjc[d] = push("pj", d, pj_all.at[0], pj_all.at[d], to)
+
+    pz, pc = {}, {}
+
+    def activate(d):
+        for copy in rz[d]:
+            copy.wait_recv()
+        if d:
+            pjc[d].wait_recv()
+        total = part[d, c, zh] + part_in[d, zh]
+        for e in (1, 2, 3):
+            total = total + red_in[e, d].astype(F32)
+        both = pj_all[d]
+        v = total[:, :384] + scaling * nn(both[:, :64], upin_ref[...])
+        grad = total[:, 384:] + scaling * nn(both[:, 64:], dout_ref[...])
+        t = jnp.tanh(coef * (v + 0.044715 * v * v * v))
+        act_all[d] = (0.5 * v * (1.0 + t)).astype(BF16)
+        slope = 0.5 * (1.0 + t) + 0.5 * v * (1.0 - t * t) * coef * (1.0 + 3.0 * 0.044715 * v * v)
+        pre[c, zh, d] = (grad * slope).astype(BF16)
+        mine = pre.at[c, zh, d]
+        pz[d] = {e: push("pz%d" % d, e, mine, mine, at_h(e)) for e in (2, 1, 3)}
+        pc[d] = [push("pc%d" % d, 0, mine, mine, other)]
+
+    def forward(d):
+        for e in (1, 3, 2):
+            pz[d][e].wait_recv()
+            got = pre.at[c, (zh + 4 - e) % 4, d]
+            pc[d].append(push("pc%d" % d, e, got, got, other))
+
+    c1 = []
+
+    def back(d):
+        for copy in pc[d]:
+            copy.wait_recv()
+        rows = jnp.concatenate([pre[0, :, d].reshape(64, 384), pre[1, :, d].reshape(64, 384)], 0)
+        value = nt(rows, w1[...]).astype(BF16)
+        dxp[0, d] = value[:64].reshape(4, 16, 768)
+        dxp[1, d] = value[64:].reshape(4, 16, 768)
+        if d:
+            e = 4 - d
+            c1.append(push("ya", e, dxp.at[0, d], c1in.at[0, e], at_y(e)))
+            c1.append(push("xb", e, dxp.at[1, d], c1in.at[1, e], at_x(e)))
+
+    for d in ORDER:
+        activate(d)
+
+    acts = act_all[...].reshape(64, 384)
+    pres = pre[c, zh].reshape(64, 384)
+    both = jnp.concatenate([nt(acts, dout_ref[...]), nt(pres, upin_ref[...])], 1).reshape(4, 16, 128)
+    for d in range(4):
+        fxb[x, oc * ((y + 4 - d) % 4) + c * ((x + 4 - d) % 4)] = both[d]
     fx = [push("fx", d, fxb.at[x], fxb.at[x], at_x(d)) for d in (2, 1, 3)]
-    eown[0] = scaling * tn(proj_in, pre_own)
-    eown[1] = scaling * tn(proj_grad, act)
+    forward(0)
+    ranks = pj_all[...].reshape(64, 128)
+    eown[0] = scaling * tn(ranks[:, :64], pres)
+    eown[1] = scaling * tn(ranks[:, 64:], acts)
     ec = push("ec", 0, eown.at[oc], ein, other)
-
+    forward(1)
     for copy in fx:
         copy.wait_recv()
     fyb[y] = fxb[0] + fxb[1] + fxb[2] + fxb[3]
     fy = [push("fy", d, fyb.at[y], fyb.at[y], at_y(d)) for d in (2, 1, 3)]
-
+    forward(3)
+    back(0)
     ec.wait_recv()
-    esum = eown[c] + ein[...]
-    ezout[...] = esum.astype(BF16).reshape(4, 16, 384)
+    ezout[...] = (eown[c] + ein[...]).astype(BF16).reshape(4, 16, 384)
     ez = [push("ez", d, ezout.at[(zh + d) % 4], ezin.at[d], at_h(d)) for d in (2, 1, 3)]
-
+    back(1)
     for copy in fy:
         copy.wait_recv()
     fzb[z] = fyb[0] + fyb[1] + fyb[2] + fyb[3]
     fz = [push("fz", d, fzb.at[z], fzb.at[z], at_z(d)) for d in (2, 1, 3)]
-
-    for d in (1, 3, 2):
-        pz[d].wait_recv()
-        got = pre.at[c, (zh + 4 - d) % 4]
-        pc.append(push("pc", d, got, got, other))
+    forward(2)
+    back(3)
+    back(2)
 
     for copy in fz:
         copy.wait_recv()
-    proj[c, zh] = (fzb[0] + fzb[1] + fzb[2] + fzb[3]).astype(BF16)
-    mine = proj.at[c, zh]
+    proj[c, :, zh] = (fzb[0] + fzb[1] + fzb[2] + fzb[3]).astype(BF16)
+    mine = proj.at[c, :, zh]
     nz = {d: push("nz", d, mine, mine, at_h(d)) for d in (2, 1, 3)}
     nc = [push("nc", 0, mine, mine, other)]
-
-    for copy in pc:
-        copy.wait_recv()
-    for h in range(2):
-        rows = pre[h].reshape(256, 384)
-        dxp[h] = nt(rows, w1[...]).astype(BF16).reshape(4, 4, 16, 768)
-    c1 = []
-    for d in (2, 1, 3):
-        c1.append(push("ya", d, dxp.at[0, (y + d) % 4], c1in.at[0, d], at_y(d)))
-        c1.append(push("xb", d, dxp.at[1, (x + d) % 4], c1in.at[1, d], at_x(d)))
 
     for copy in ez:
         copy.wait_recv()
@@ -219,8 +267,8 @@
     for copy in c1:
         copy.wait_recv()
     c2 = []
-    s0 = dxp[0, y].astype(F32)
-    s1 = dxp[1, x].astype(F32)
+    s0 = dxp[0, 0].astype(F32)
+    s1 = dxp[1, 0].astype(F32)
     for d in (1, 2, 3):
         s0 = s0 + c1in[0, d].astype(F32)
         s1 = s1 + c1in[1, d].astype(F32)
@@ -232,7 +280,7 @@
 
     for d in (1, 3, 2):
         nz[d].wait_recv()
-        got = proj.at[c, (zh + 4 - d) % 4]
+        got = proj.at[c, :, (zh + 4 - d) % 4]
         nc.append(push("nc", d, got, got, other))
 
     for copy in c2:
@@ -267,11 +315,11 @@
     gdout_ref[...] = egb[1].reshape(64, 384).astype(F32)
 
     half = z // 2
-    k = jnp.where(half == 0, y, x)
-    j = jnp.where(half == 0, x, y)
-    rows = proj[half, k, pl.ds(pl.multiple_of(j * 16, 16), 16), :].astype(F32)
-    back = jnp.where(z % 2 == 0, rows[:8], rows[8:])[:, 64:].astype(BF16)
-    extra = scaling * nn(back, din_ref[...])
+    k = (1 - half) * y + half * x
+    j = (1 - half) * x + half * y
+    rows = proj[half, k, j].astype(F32)
+    own = jnp.where(z % 2 == 0, rows[:8], rows[8:])[:, 64:].astype(BF16)
+    extra = scaling * nn(own, din_ref[...])
     for copy in cz:
         copy.wait_recv()
     out = czout[z] + extra
@@ -323,16 +371,21 @@
             pltpu.VMEM((64, 768), BF16),
             pltpu.VMEM((4, 16, 768), BF16),
             pltpu.VMEM((2, 4, 2, 4, 16, 768), BF16),
-            pltpu.VMEM((4, 64, 896), F32),
-            pltpu.VMEM((4, 64, 896), F32),
-            pltpu.VMEM((4, 64, 896), F32),
-            pltpu.VMEM((4, 64, 896), BF16),
-            pltpu.VMEM((4, 64, 896), BF16),
-            pltpu.VMEM((2, 4, 64, 384), BF16),
-            pltpu.VMEM((2, 4, 64, 128), BF16),
-            pltpu.VMEM((4, 64, 128), F32),
-            pltpu.VMEM((4, 64, 128), F32),
-            pltpu.VMEM((4, 64, 128), F32),
+            pltpu.VMEM((4, 2, 4, 16, 768), F32),
+            pltpu.VMEM((4, 4, 16, 768), F32),
+            pltpu.VMEM((2, 4, 16, 128), F32),
+            pltpu.VMEM((4, 16, 128), F32),
+            pltpu.VMEM((4, 4, 16, 768), BF16),
+            pltpu.VMEM((4, 4, 16, 768), BF16),
+            pltpu.VMEM((4, 16, 128), BF16),
+            pltpu.VMEM((4, 16, 128), BF16),
+            pltpu.VMEM((4, 16, 128), BF16),
+            pltpu.VMEM((4, 16, 384), BF16),
+            pltpu.VMEM((2, 4, 4, 16, 384), BF16),
+            pltpu.VMEM((2, 4, 4, 16, 128), BF16),
+            pltpu.VMEM((4, 4, 16, 128), F32),
+            pltpu.VMEM((4, 4, 16, 128), F32),
+            pltpu.VMEM((4, 4, 16, 128), F32),
             pltpu.VMEM((2, 64, 384), F32),
             pltpu.VMEM((64, 384), F32),
             pltpu.VMEM((4, 16, 384), BF16),

time: 95.5 us -> 85.1 us (0.89)
  Pallas kernels: 94.5 us -> 84.2 us
    pallas_call x1, Pallas kernels: 92.6 us -> 82.3 us  [shards(): pl.pallas_call(kernel, out_shape=shapes, in_specs=[hbm] * 8, out_specs=(v...]
where the time goes in v4:
time: 85.1 us; the launch traced here: 84.8 us
  Pallas kernels  84.2 us (99%)
    pallas_call x1, Pallas kernels, shards(): pl.pallas_call(kernel, out_shape=shapes, in_specs=[hbm] * 8, out_specs=(v...  82.3 us
    pallas_call x1, Pallas kernels, shards(): pl.pallas_call(hand_over, out_shape=shapes, in_specs=[hbm] * 5, out_specs...  1.9 us

profile of v4, /device:TPU:1, one launch (start us, length us, event | category | flops | bytes accessed | tf_op | source)
XLA Modules:
  0.0 84.8 jit_solution(7320830041568579582)
XLA Ops:
  0.6 82.3 %shard_map.119 = (bf16[8,768]{1,0:T(8,128)(2,1)}, f32[64,768]{1,0:T(8,128)}, f32[64,384]{1,0:T(8,128)}, f32[64,384]{1,0:T(8,128)}, f32[64,768]{1,0:T(8,128)}) custom-call(bf16[8,768]{1,0:T(8,128)(2,1)} %x_hbm.1, bf16[8,768]{1,0:T(8,128)(2,1)} %g_hbm.1, bf16[768,384]{1,0:T(8,128)(2,1)} %w1_hbm.1, bf16[384,768]{1,0:T(8,128)(2,1)} %w2_hbm.1, ...), custom_call_target="tpu_custom_call" | custom-call | tf_op jit(solution)/shard_map/pallas_call | solution.py:358
  83.0 1.9 %shard_map.120 = (bf16[8,768]{1,0:T(8,128)(2,1)}, f32[64,768]{1,0:T(8,128)}, f32[64,384]{1,0:T(8,128)}, f32[64,384]{1,0:T(8,128)}, f32[64,768]{1,0:T(8,128)}) custom-call(bf16[8,768]{1,0:T(8,128)(2,1)} %get-tuple-element.10.refs_0_, f32[64,768]{1,0:T(8,128)} %get-tuple-element.11.refs_1_, f32[64,384]{1,0:T(8,128)} %get-tuple-element.12.refs_2_, ...), custom_call_target="tpu_custom_call" | custom-call | tf_op jit(solution)/shard_map/pallas_call | solution.py:408

commit v5 on v4

--- a/solution.py
+++ b/solution.py
@@ -15,7 +15,7 @@
 coef = math.sqrt(2.0 / math.pi)
 
 FAMILIES = (
-    "gz", "ga", "gb", "gc", "gd", "core", "cj", "rz0", "rz1", "rz2", "rz3", "rj", "pj",
+    "gz", "ga", "gb", "gc", "gd", "gf", "gh", "core", "cj", "rz0", "rz1", "rz2", "rz3", "rj", "pj",
     "pz0", "pz1", "pz2", "pz3", "pc0", "pc1", "pc2", "pc3", "fx", "fy", "fz", "nz", "nc",
     "ec", "ez", "eg", "eh", "ya", "xa", "xb", "yb", "cz",
 )
@@ -37,12 +37,12 @@
 
 def kernel(
     x_hbm, g_hbm, w1_hbm, w2_hbm, din_hbm, upin_hbm, dout_hbm, upout_hbm,
-    dx_ref, gdin_ref, gupin_ref, gdout_ref, gupout_ref,
+    dx_hbm, gdin_hbm, gupin_hbm, gdout_hbm, gupout_hbm,
     x_ref, g_ref, w1, w2, din_ref, upin_ref, dout_ref, upout_ref,
     zbuf, strip, part, part_in, pj, pj_in, red_out, red_in, pj_out, pj_red, pj_all,
     act_all, pre, proj, fxb, fyb, fzb, eown, ein, ezout, ezin, egb,
     dxp, c1in, c2out, c2in, czout, czin,
-    wsem, ssem, rsem,
+    dx_ref, gdin_ref, gupin_ref, gdout_ref, gupout_ref, wsem, osem, ssem, rsem,
 ):
     w = lax.axis_index("wide")
     n = lax.axis_index("narrow")
@@ -64,6 +64,10 @@
 
     other = (w, zh * 2 + oc)
     sent = []
+
+    def drain():
+        while sent:
+            sent.pop(0).wait_send()
 
     def push(family, slot, src, dst, to):
         i = FAMILY[family]
@@ -74,6 +78,13 @@
         copy.start()
         sent.append(copy)
         return copy
+
+    outs = []
+
+    def save(i, src, dst):
+        copy = pltpu.make_async_copy(src, dst, osem.at[i])
+        copy.start()
+        outs.append(copy)
 
     loads = [
         pltpu.make_async_copy(src, dst, wsem.at[i])
@@ -113,7 +124,7 @@
     for copy in copies:
         copy.wait_recv()
     gc, gd = {}, {}
-    for d in (1, 3, 2):
+    for d in (1, 3):
         mine = strip.at[0, y]
         gc[d] = push("gc", d, mine, mine, at_y(d))
         mine = strip.at[1, x]
@@ -124,9 +135,6 @@
     core = {}
 
     def multiply(d):
-        if d:
-            gc[d].wait_recv()
-            gd[d].wait_recv()
         ka, kb = (y + 4 - d) % 4, (x + 4 - d) % 4
         xs = jnp.concatenate([strip[0, ka, 0].reshape(64, 768), strip[1, kb, 0].reshape(64, 768)], 0)
         gs = jnp.concatenate([strip[0, ka, 1].reshape(64, 768), strip[1, kb, 1].reshape(64, 768)], 0)
@@ -158,10 +166,23 @@
                 push("rj", e, pj_out.at[(zh + e) % 4], pj_red.at[e], at_h(e)) for e in (2, 1, 3)
             ]
 
-    for d in ORDER:
-        multiply(d)
-        scatter(d)
-
+    multiply(0)
+    scatter(0)
+    far = []
+    for t, d in ((0, 1), (1, 3)):
+        gc[d].wait_recv()
+        got = strip.at[0, (y + 4 - d) % 4, t]
+        far.append(push("gf", d, got, got, at_y(d)))
+        gd[d].wait_recv()
+        got = strip.at[1, (x + 4 - d) % 4, t]
+        far.append(push("gh", d, got, got, at_x(d)))
+    multiply(1)
+    multiply(3)
+    scatter(1)
+    scatter(3)
+    for copy in far:
+        copy.wait_recv()
+    multiply(2)
     for copy in rz["j"]:
         copy.wait_recv()
     total = pj[c, zh] + pj_in[zh]
@@ -172,6 +193,7 @@
     for d in (2, 1, 3):
         to = (oc * at_y(d)[0] + c * at_x(d)[0], n)
         pjc[d] = push("pj", d, pj_all.at[0], pj_all.at[d], to)
+    scatter(2)
 
     pz, pc = {}, {}
 
@@ -223,26 +245,27 @@
     for d in range(4):
         fxb[x, oc * ((y + 4 - d) % 4) + c * ((x + 4 - d) % 4)] = both[d]
     fx = [push("fx", d, fxb.at[x], fxb.at[x], at_x(d)) for d in (2, 1, 3)]
-    forward(0)
     ranks = pj_all[...].reshape(64, 128)
     eown[0] = scaling * tn(ranks[:, :64], pres)
     eown[1] = scaling * tn(ranks[:, 64:], acts)
     ec = push("ec", 0, eown.at[oc], ein, other)
-    forward(1)
+    forward(0)
     for copy in fx:
         copy.wait_recv()
     fyb[y] = fxb[0] + fxb[1] + fxb[2] + fxb[3]
     fy = [push("fy", d, fyb.at[y], fyb.at[y], at_y(d)) for d in (2, 1, 3)]
-    forward(3)
+    forward(1)
     back(0)
     ec.wait_recv()
     ezout[...] = (eown[c] + ein[...]).astype(BF16).reshape(4, 16, 384)
     ez = [push("ez", d, ezout.at[(zh + d) % 4], ezin.at[d], at_h(d)) for d in (2, 1, 3)]
-    back(1)
     for copy in fy:
         copy.wait_recv()
     fzb[z] = fyb[0] + fyb[1] + fyb[2] + fyb[3]
     fz = [push("fz", d, fzb.at[z], fzb.at[z], at_z(d)) for d in (2, 1, 3)]
+    forward(3)
+    back(1)
+    drain()
     forward(2)
     back(3)
     back(2)
@@ -307,12 +330,16 @@
     xs = strip[:, :, 0].reshape(512, 768)
     gs = strip[:, :, 1].reshape(512, 768)
     gupout_ref[...] = scaling * tn(rank[:, :64], gs)
+    save(0, gupout_ref, gupout_hbm)
     gdin_ref[...] = scaling * tn(rank[:, 64:], xs)
+    save(1, gdin_ref, gdin_hbm)
 
     for copy in eh:
         copy.wait_recv()
     gupin_ref[...] = egb[0].reshape(64, 384).astype(F32)
     gdout_ref[...] = egb[1].reshape(64, 384).astype(F32)
+    save(2, gupin_ref, gupin_hbm)
+    save(3, gdout_ref, gdout_hbm)
 
     half = z // 2
     k = (1 - half) * y + half * x
@@ -326,9 +353,11 @@
     for d in (1, 2, 3):
         out = out + czin[d]
     dx_ref[...] = out.astype(BF16)
-
-    for copy in sent:
-        copy.wait_send()
+    save(4, dx_ref, dx_hbm)
+
+    drain()
+    for copy in outs:
+        copy.wait()
 
 
 def hand_over(*refs):
@@ -345,7 +374,6 @@
 
 
 def shards(x, g, w1, w2, din, upin, dout, upout):
-    vmem = pl.BlockSpec(memory_space=pltpu.VMEM)
     hbm = pl.BlockSpec(memory_space=pl.ANY)
     nf = len(FAMILIES)
     shapes = (
@@ -359,7 +387,7 @@
         kernel,
         out_shape=shapes,
         in_specs=[hbm] * 8,
-        out_specs=(vmem,) * 5,
+        out_specs=(hbm,) * 5,
         scratch_shapes=[
             pltpu.VMEM((8, 768), BF16),
             pltpu.VMEM((8, 768), BF16),
@@ -397,7 +425,11 @@
             pltpu.VMEM((2, 4, 16, 768), F32),
             pltpu.VMEM((4, 8, 768), F32),
             pltpu.VMEM((4, 8, 768), F32),
+        ]
+        + [pltpu.VMEM(t.shape, t.dtype) for t in shapes]
+        + [
             pltpu.SemaphoreType.DMA((8,)),
+            pltpu.SemaphoreType.DMA((5,)),
             pltpu.SemaphoreType.DMA((nf, 4)),
             pltpu.SemaphoreType.DMA((nf, 4)),
         ],

time: 85.1 us -> 85.6 us (level)
  no operation moved by 1% of the time
where the time goes in v5:
time: 85.6 us; the launch traced here: 85.3 us
  Pallas kernels  84.7 us (99%)
    pallas_call x1, Pallas kernels, shards(): pl.pallas_call(kernel, out_shape=shapes, in_specs=[hbm] * 8, out_specs=(h...  82.8 us
    pallas_call x1, Pallas kernels, shards(): pl.pallas_call(hand_over, out_shape=shapes, in_specs=[hbm] * 5, out_specs...  1.9 us

profile of v5, /device:TPU:1, one launch (start us, length us, event | category | flops | bytes accessed | tf_op | source)
XLA Modules:
  0.0 85.3 jit_solution(9303952843025877693)
XLA Ops:
  0.6 82.8 %shard_map.119 = (bf16[8,768]{1,0:T(8,128)(2,1)}, f32[64,768]{1,0:T(8,128)}, f32[64,384]{1,0:T(8,128)}, f32[64,384]{1,0:T(8,128)}, f32[64,768]{1,0:T(8,128)}) custom-call(bf16[8,768]{1,0:T(8,128)(2,1)} %x_hbm.1, bf16[8,768]{1,0:T(8,128)(2,1)} %g_hbm.1, bf16[768,384]{1,0:T(8,128)(2,1)} %w1_hbm.1, bf16[384,768]{1,0:T(8,128)(2,1)} %w2_hbm.1, ...), custom_call_target="tpu_custom_call" | custom-call | tf_op jit(solution)/shard_map/pallas_call | solution.py:386
  83.4 1.9 %shard_map.120 = (bf16[8,768]{1,0:T(8,128)(2,1)}, f32[64,768]{1,0:T(8,128)}, f32[64,384]{1,0:T(8,128)}, f32[64,384]{1,0:T(8,128)}, f32[64,768]{1,0:T(8,128)}) custom-call(bf16[8,768]{1,0:T(8,128)(2,1)} %get-tuple-element.10.refs_0_, f32[64,768]{1,0:T(8,128)} %get-tuple-element.11.refs_1_, f32[64,384]{1,0:T(8,128)} %get-tuple-element.12.refs_2_, ...), custom_call_target="tpu_custom_call" | custom-call | tf_op jit(solution)/shard_map/pallas_call | solution.py:440

commit v6 on v5

--- a/solution.py
+++ b/solution.py
@@ -261,7 +261,7 @@
     ez = [push("ez", d, ezout.at[(zh + d) % 4], ezin.at[d], at_h(d)) for d in (2, 1, 3)]
     for copy in fy:
         copy.wait_recv()
-    fzb[z] = fyb[0] + fyb[1] + fyb[2] + fyb[3]
+    fzb[z] = (fyb[0] + fyb[1] + fyb[2] + fyb[3]).astype(BF16)
     fz = [push("fz", d, fzb.at[z], fzb.at[z], at_z(d)) for d in (2, 1, 3)]
     forward(3)
     back(1)
@@ -272,7 +272,7 @@
 
     for copy in fz:
         copy.wait_recv()
-    proj[c, :, zh] = (fzb[0] + fzb[1] + fzb[2] + fzb[3]).astype(BF16)
+    proj[c, :, zh] = sum(fzb[i].astype(F32) for i in range(4)).astype(BF16)
     mine = proj.at[c, :, zh]
     nz = {d: push("nz", d, mine, mine, at_h(d)) for d in (2, 1, 3)}
     nc = [push("nc", 0, mine, mine, other)]
@@ -295,8 +295,8 @@
     for d in (1, 2, 3):
         s0 = s0 + c1in[0, d].astype(F32)
         s1 = s1 + c1in[1, d].astype(F32)
-    c2out[0] = s0
-    c2out[1] = s1
+    c2out[0] = s0.astype(BF16)
+    c2out[1] = s1.astype(BF16)
     for d in (2, 1, 3):
         c2.append(push("xa", d, c2out.at[0, (x + d) % 4], c2in.at[0, d], at_x(d)))
         c2.append(push("yb", d, c2out.at[1, (y + d) % 4], c2in.at[1, d], at_y(d)))
@@ -308,11 +308,11 @@
 
     for copy in c2:
         copy.wait_recv()
-    s0 = c2out[0, x]
-    s1 = c2out[1, y]
+    s0 = c2out[0, x].astype(F32)
+    s1 = c2out[1, y].astype(F32)
     for d in (1, 2, 3):
-        s0 = s0 + c2in[0, d]
-        s1 = s1 + c2in[1, d]
+        s0 = s0 + c2in[0, d].astype(F32)
+        s1 = s1 + c2in[1, d].astype(F32)
     czout[0] = s0[:8]
     czout[1] = s0[8:]
     czout[2] = s1[:8]
@@ -413,7 +413,7 @@
             pltpu.VMEM((2, 4, 4, 16, 128), BF16),
             pltpu.VMEM((4, 4, 16, 128), F32),
             pltpu.VMEM((4, 4, 16, 128), F32),
-            pltpu.VMEM((4, 4, 16, 128), F32),
+            pltpu.VMEM((4, 4, 16, 128), BF16),
             pltpu.VMEM((2, 64, 384), F32),
             pltpu.VMEM((64, 384), F32),
             pltpu.VMEM((4, 16, 384), BF16),
@@ -421,8 +421,8 @@
             pltpu.VMEM((2, 4, 16, 384), BF16),
             pltpu.VMEM((2, 4, 4, 16, 768), BF16),
             pltpu.VMEM((2, 4, 4, 16, 768), BF16),
-            pltpu.VMEM((2, 4, 16, 768), F32),
-            pltpu.VMEM((2, 4, 16, 768), F32),
+            pltpu.VMEM((2, 4, 16, 768), BF16),
+            pltpu.VMEM((2, 4, 16, 768), BF16),
             pltpu.VMEM((4, 8, 768), F32),
             pltpu.VMEM((4, 8, 768), F32),
         ]

time: 85.6 us -> 84.8 us (level)
  Pallas kernels: 84.7 us -> 83.8 us
where the time goes in v6:
time: 84.8 us; the launch traced here: 84.5 us
  Pallas kernels  83.8 us (99%)
    pallas_call x1, Pallas kernels, shards(): pl.pallas_call(kernel, out_shape=shapes, in_specs=[hbm] * 8, out_specs=(h...  81.9 us
    pallas_call x1, Pallas kernels, shards(): pl.pallas_call(hand_over, out_shape=shapes, in_specs=[hbm] * 5, out_specs...  1.9 us

profile of v6, /device:TPU:1, one launch (start us, length us, event | category | flops | bytes accessed | tf_op | source)
XLA Modules:
  0.0 84.5 jit_solution(1698888994516602832)
XLA Ops:
  0.6 81.9 %shard_map.119 = (bf16[8,768]{1,0:T(8,128)(2,1)}, f32[64,768]{1,0:T(8,128)}, f32[64,384]{1,0:T(8,128)}, f32[64,384]{1,0:T(8,128)}, f32[64,768]{1,0:T(8,128)}) custom-call(bf16[8,768]{1,0:T(8,128)(2,1)} %x_hbm.1, bf16[8,768]{1,0:T(8,128)(2,1)} %g_hbm.1, bf16[768,384]{1,0:T(8,128)(2,1)} %w1_hbm.1, bf16[384,768]{1,0:T(8,128)(2,1)} %w2_hbm.1, ...), custom_call_target="tpu_custom_call" | custom-call | tf_op jit(solution)/shard_map/pallas_call | solution.py:386
  82.6 1.9 %shard_map.120 = (bf16[8,768]{1,0:T(8,128)(2,1)}, f32[64,768]{1,0:T(8,128)}, f32[64,384]{1,0:T(8,128)}, f32[64,384]{1,0:T(8,128)}, f32[64,768]{1,0:T(8,128)}) custom-call(bf16[8,768]{1,0:T(8,128)(2,1)} %get-tuple-element.10.refs_0_, f32[64,768]{1,0:T(8,128)} %get-tuple-element.11.refs_1_, f32[64,384]{1,0:T(8,128)} %get-tuple-element.12.refs_2_, ...), custom_call_target="tpu_custom_call" | custom-call | tf_op jit(solution)/shard_map/pallas_call | solution.py:440
